TPU v7x, 32 devices: a whole 2x2x4 slice. The times are simulated.
32 devices in a mesh: ed: 8 (over z, core), ep: 4 (over y, x).
Axes of the slice: x: 2, y: 2, z: 4, core: 2. Of those that a mesh axis runs over, the one named last changes fastest.
Arguments:
- out_grad: bfloat16 [4096, 3584], P(('ed', 'ep')), may hold values from -4.1 to 4.1
- routes: int32 [4096, 2], P(('ed', 'ep')), may hold values from 0 to 3, all different within a row; in each aligned block of 128 rows (0 to 127, 128 to 255, ...) at most 128 rows name the same one
- gates: bfloat16 [4096, 2], P(('ed', 'ep')), may hold values from 0.049804688 to 0.59765625
- pre_acts: bfloat16 [8, 4, 4, 128, 2048], P('ed', 'ep'), may hold values from -6 to 6
- down_weight: bfloat16 [4, 1024, 3584], P('ep'), may hold values from -0.1875 to 0.1875
- history: float32 [8, 4, 16], P('ed', 'ep'), may hold values from 4 to 32
Outputs:
- pre_grad: bfloat16 [8, 4, 4, 128, 2048], P('ed', 'ep')
- wgrad: float32 [4, 3584, 1024], P('ep', 'ed')
- new_history: float32 [4, 16], P('ep')
- gate_grad: float32 [4096, 2], P(('ed', 'ep'))
Inputs may be any that keep to these rules, and one draw needn't show every extreme that they name: `routes`: each token names 2 different experts; among the 128 rows of one device no expert is named more than 128 times, and in some device's rows one expert is named exactly 128 times.
All inputs are finite; a program needn't handle non-finite values.
Results may differ from a plain program's by a relative error of at most 0.025.
Values may be sent and summed in bfloat16 or wider, within the bound.
A program may use at most 128 MiB of HBM per device.

v0:
```python
import jax
import jax.numpy as jnp
from jax import lax
from jax.sharding import PartitionSpec as P


def split_pre(pre_block, width_ff):
    gate_pre = pre_block[:, :width_ff].astype(jnp.float32)
    up_pre = pre_block[:, width_ff:].astype(jnp.float32)
    return (gate_pre, up_pre, jax.nn.sigmoid(gate_pre))


def body(out_grad, routes, gates, pre_acts, down_weight, history):
    tok_rows, top = routes.shape
    width = out_grad.shape[1]
    local = down_weight.shape[0]
    width_ff = down_weight.shape[1]
    n_src = pre_acts.shape[2]
    cap = pre_acts.shape[3]
    n_ep = lax.axis_size("ep")
    n_replicas = lax.axis_size("ed")
    experts = local * n_ep
    flat = routes.reshape(-1)
    hits = (flat[:, None] == jnp.arange(experts, dtype=jnp.int32)[None, :]).astype(jnp.int32)
    before = jnp.cumsum(hits, axis=0) - hits
    slot = jnp.sum(before * hits, axis=1)
    target = flat * cap + slot
    owner = jnp.arange(tok_rows * top, dtype=jnp.int32) // top
    table = jnp.zeros((experts * cap,), jnp.int32).at[target].set(owner + 1)
    picked = out_grad[jnp.maximum(table - 1, 0)]
    send_rows = jnp.where((table > 0)[:, None], picked, jnp.zeros_like(picked))
    send_gate = jnp.zeros((experts * cap,), jnp.bfloat16).at[target].set(gates.reshape(-1))
    arrived, arrived_gate = (
        lax.all_to_all(
            send_rows.reshape(n_ep, local * cap, width),
            "ep",
            split_axis=0,
            concat_axis=0,
            tiled=True,
        ),
        lax.all_to_all(
            send_gate.reshape(n_ep, local * cap), "ep", split_axis=0, concat_axis=0, tiled=True
        ),
    )
    arrived = (
        arrived.reshape(n_ep, local, cap, width)
        .transpose(1, 0, 2, 3)
        .reshape(local, n_ep * cap, width)
    )
    arrived_gate = (
        arrived_gate.reshape(n_ep, local, cap)
        .transpose(1, 0, 2)
        .reshape(local, n_ep * cap)
        .astype(jnp.float32)
    )
    merged = lax.pmax(history, "ed")[0]
    ref_amax = jnp.max(merged, axis=1)
    scale = 1.0 / ref_amax
    rows = arrived[0]
    gate_row = arrived_gate[0][:, None]
    weight = down_weight[0]
    pre_block = pre_acts[0, 0].reshape(n_src * cap, 2 * width_ff)
    gate_pre, up_pre, sigma = split_pre(pre_block, width_ff)
    act = (gate_pre * sigma * up_pre).astype(jnp.bfloat16)
    weighted = (gate_row * act.astype(jnp.float32)).astype(jnp.bfloat16)
    raw = jnp.einsum("rd,hd->rh", rows, weight, preferred_element_type=jnp.float32)
    score = jnp.sum(act.astype(jnp.float32) * raw, axis=1)
    grad_act = gate_row * raw
    grad_gate = grad_act * up_pre * sigma * (1.0 + gate_pre * (1.0 - sigma))
    grad_up = grad_act * gate_pre * sigma
    grads_pre = [
        jnp.concatenate([grad_gate, grad_up], axis=1)
        .astype(jnp.bfloat16)
        .reshape(n_src, cap, 2 * width_ff)
    ]
    scores = [score.reshape(n_ep, cap)]
    factor = scale[0]

    def term(start, count, rows=rows, weighted=weighted, factor=factor):
        return factor * jnp.einsum("rd,rh->dh", rows, weighted, preferred_element_type=jnp.float32)

    shard = lax.psum_scatter(
        term(jnp.int32(0), width // n_replicas * lax.axis_size("ed")).astype(jnp.bfloat16),
        "ed",
        scatter_dimension=0,
        tiled=True,
    ).astype(jnp.float32)
    shards = [shard]
    wgrad = jnp.stack(shards)
    peak = lax.pmax(jnp.max(jnp.abs(wgrad), axis=(1, 2)), "ed")
    new_amax = peak * ref_amax
    new_history = jnp.concatenate([merged[:, 1:], new_amax[:, None]], axis=1)
    pre_grad = jnp.stack(grads_pre)[None]
    outgoing = jnp.stack(scores).transpose(1, 0, 2).reshape(n_ep, local * cap)
    returned = lax.all_to_all(outgoing, "ep", split_axis=0, concat_axis=0, tiled=True)
    gate_grad = returned.reshape(-1)[target].reshape(tok_rows, top)
    return (pre_grad, wgrad, new_history, gate_grad)


def solution(mesh):
    placed = (
        P(("ed", "ep"), None),
        P(("ed", "ep"), None),
        P(("ed", "ep"), None),
        P("ed", "ep", None, None, None),
        P("ep", None, None),
        P("ed", "ep", None),
    )
    return jax.shard_map(
        body,
        mesh=mesh,
        in_specs=placed,
        out_specs=(
            P("ed", "ep", None, None, None),
            P("ep", "ed", None),
            P("ep", None),
            P(("ed", "ep"), None),
        ),
        check_vma=False,
    )
```

profile of v0, /device:TPU:0, one launch (start us, length us, event | category | flops | bytes accessed | tf_op | source)
XLA Modules:
  0.0 192.5 jit_solution(8770633594050907044)
XLA Ops:
  7.2 0.0 copy-start
  7.2 0.8 broadcast_multiply_fusion
  7.9 0.8 copy.20
  8.7 0.1 eq.29
  8.9 0.1 eq.25
  9.0 0.8 copy.24
  9.8 0.1 reshape.149
  9.9 0.1 copy.19
  10.1 0.1 mul.71
  10.2 1.2 reduce-window.6
  11.4 0.1 slice.24
  11.5 0.1 copy.22
  11.7 0.1 copy.23
  11.8 0.1 add_bitcast_fusion
  11.9 2.2 %scatter_custom_fusion = bf16[512]{0:T(512)(128)(2,1)S(1)} fusion(s32[256]{0:T(256)S(1)} %bitcast.52, bf16[256]{0:T(256)(128)(2,1)S(1)} %reshape.149, bf16[]{:T(256)} %constant.15.clone.1), kind=kCustom, calls=%fused_computation.54 | custom fusion | bytes 1026 | tf_op jit(solution)/shard_map/scatter | solution.py:32
  14.0 0.6 copy.25
  14.6 5.2 %all-to-all-start = ((bf16[4,1,128]{2,1,0:T(2,128)(2,1)}), bf16[4,1,128]{2,1,0:T(2,128)(2,1)S(1)}, u32[]{:S(2)}, u32[]{:S(2)}) async-start(bf16[4,1,128]{2,1,0:T(2,128)(2,1)} %copy.25), calls=%async_computation | async-start | bytes 4096 | tf_op jit(solution)/shard_map/all_to_all | solution.py:41
  19.8 1.4 scatter_custom_fusion.1
  21.2 0.0 copy-done
  21.2 4.2 %gather_fusion = bf16[512,3584]{1,0:T(8,128)(2,1)} fusion(bf16[128,3584]{1,0:T(8,128)(2,1)S(1)} %copy-done, s32[1024]{0:T(1024)S(1)} %pad_clamp_fusion.1), kind=kCustom, calls=%fused_computation | custom fusion | bytes 7342080 | tf_op jit(solution)/shard_map/gather | solution.py:30
  25.5 4.1 %broadcast_select_fusion = bf16[4,128,3584]{2,1,0:T(8,128)(2,1)} fusion(bf16[4,128,3584]{2,1,0:T(8,128)(2,1)} %bitcast.49, pred[4,128]{1,0:T(4,128)(4,1)S(1)} %compare_bitcast_fusion), kind=kLoop, calls=%fused_computation.11 | loop fusion | flops 1835008 | bytes 7340544 | tf_op jit(solution)/shard_map/jit(_where)/select_n | solution.py:31
  29.6 0.0 copy-start.2
  29.6 0.0 copy-start.1
  29.6 0.0 all-to-all-done
  29.6 4.9 %all-to-all-start.1 = ((bf16[4,128,3584]{2,1,0:T(8,128)(2,1)}), bf16[4,128,3584]{2,1,0:T(8,128)(2,1)}, u32[]{:S(2)}, u32[]{:S(2)}) async-start(bf16[4,128,3584]{2,1,0:T(8,128)(2,1)} %broadcast_select_fusion), calls=%async_computation.1 | async-start | bytes 7340032 | tf_op jit(solution)/shard_map/all_to_all | solution.py:34
  34.5 0.0 reduce-scatter.2.cloned.1.call-start
  34.5 0.0 copy-done.2
  34.5 16.3 %pmax.14 = f32[1,1,16]{2,1,0:T(1,128)S(1)} all-reduce(f32[1,1,16]{2,1,0:T(1,128)S(1)} %copy-done.2), channel_id=1, replica_groups=mesh['ed'=8,'ep'=4] {'ed'}, use_global_device_ids=true, to_apply=%region_5.6 | all-reduce | flops 16 | bytes 128 | tf_op jit(solution)/shard_map/pmax | solution.py:56
  50.9 0.6 reduce_max.22
  52.2 24.1 %all-to-all-done.1 = bf16[4,128,3584]{2,1,0:T(8,128)(2,1)} async-done(((bf16[4,128,3584]{2,1,0:T(8,128)(2,1)}), bf16[4,128,3584]{2,1,0:T(8,128)(2,1)}, u32[]{:S(2)}, u32[]{:S(2)}) %all-to-all-start.1) | async-done | bytes 3670048 | tf_op jit(solution)/shard_map/all_to_all | solution.py:34
  76.3 0.0 copy-done.1
  76.3 8.5 %multiply_convert_fusion = bf16[3584,1024]{1,0:T(8,128)(2,1)} fusion(bf16[512,3584]{1,0:T(8,128)(2,1)} %bitcast.8, f32[]{:T(128)} %bitcast.14, f32[512]{0:T(512)S(1)} %bitcast.57, bf16[512,2048]{1,0:T(8,128)(2,1)S(1)} %bitcast.61), kind=kOutput, calls=%fused_computation.4 | convolution fusion | flops 3771203584 | bytes 13109252 | tf_op jit(solution)/shard_map/rd,rh->dh/dot_general | solution.py:80
  84.9 0.0 reduce-scatter.2.cloned.1.call-update
  84.9 0.1 slice.19
  85.0 10.3 %fusion.4 = (bf16[512,1024]{1,0:T(8,128)(2,1)S(1)}, bf16[512,1024]{1,0:T(8,128)(2,1)S(1)}, f32[512]{0:T(512)}) fusion(f32[512]{0:T(512)S(1)} %bitcast.58, bf16[512,2048]{1,0:T(8,128)(2,1)} %bitcast.60, bf16[512,3584]{1,0:T(8,128)(2,1)} %bitcast.8, bf16[1,1024,3584]{2,1,0:T(8,128)(2,1)} %param.10), kind=kOutput, calls=%fused_computation.20 | convolution fusion | flops 3769630208 | bytes 15208448 | tf_op jit(solution)/shard_map/rd,hd->rh/dot_general | solution.py:66
  95.2 3.2 %all-to-all-start.2 = ((f32[4,1,128]{2,1,0:T(1,128)}), f32[4,1,128]{2,1,0:T(1,128)S(1)}, u32[]{:S(2)}, u32[]{:S(2)}) async-start(f32[4,1,128]{2,1,0:T(1,128)} %bitcast.19), calls=%async_computation.3 | async-start | bytes 4096 | tf_op jit(solution)/shard_map/all_to_all | solution.py:95
  98.5 1.5 pad_maximum_fusion
  100.0 3.0 %all-to-all-done.2 = f32[4,1,128]{2,1,0:T(1,128)S(1)} async-done(((f32[4,1,128]{2,1,0:T(1,128)}), f32[4,1,128]{2,1,0:T(1,128)S(1)}, u32[]{:S(2)}, u32[]{:S(2)}) %all-to-all-start.2) | async-done | bytes 2080 | tf_op jit(solution)/shard_map/all_to_all | solution.py:95
  103.0 1.9 %gather_fusion.1 = f32[256]{0:T(256)S(1)} fusion(f32[512]{0:T(512)S(1)} %bitcast.48, s32[1024]{0:T(1024)S(1)} %pad_clamp_fusion), kind=kCustom, calls=%fused_computation.1 | custom fusion | bytes 3072 | tf_op jit(solution)/shard_map/gather | solution.py:96
  105.0 0.1 reshape.127
  105.1 0.6 copy.26
  105.7 59.3 %reduce-scatter.2.cloned.1.call-done = bf16[448,1024]{1,0:T(8,128)(2,1)} async-done(((bf16[3584,1024]{1,0:T(8,128)(2,1)}), bf16[448,1024]{1,0:T(8,128)(2,1)}) %reduce-scatter.2.cloned.1.call-update) | async-done | bytes 917520 | tf_op jit(solution)/shard_map/reduce_scatter | solution.py:82
  165.0 1.9 fusion.14
  166.9 14.2 %pmax.15 = f32[1]{0:T(128)} all-reduce(f32[1]{0:T(128)} %bitcast.17), channel_id=1, replica_groups=mesh['ed'=8,'ep'=4] {'ed'}, use_global_device_ids=true, to_apply=%region_9.10 | all-reduce | flops 1 | bytes 8 | tf_op jit(solution)/shard_map/pmax | solution.py:90
  182.4 0.6 pad_maximum_fusion.1
  183.0 2.6 %convert_bitcast_fusion = f32[1,448,1024]{2,1,0:T(8,128)} fusion(bf16[448,1024]{1,0:T(8,128)(2,1)} %reduce-scatter.2.cloned.1.call-done), kind=kLoop, calls=%fused_computation.17 | loop fusion | flops 458752 | bytes 2752512 | tf_op jit(solution)/shard_map/stack | solution.py:89
  (11 shorter events, 0.1 us)
Async XLA Ops:
  7.2 14.1 %copy-start = (bf16[128,3584]{1,0:T(8,128)(2,1)S(1)}, bf16[128,3584]{1,0:T(8,128)(2,1)}, u32[]{:S(2)}) copy-start(bf16[128,3584]{1,0:T(8,128)(2,1)} %param.6) | copy-start | bytes 2752516
  14.6 15.0 %all-to-all-start = ((bf16[4,1,128]{2,1,0:T(2,128)(2,1)}), bf16[4,1,128]{2,1,0:T(2,128)(2,1)S(1)}, u32[]{:S(2)}, u32[]{:S(2)}) async-start(bf16[4,1,128]{2,1,0:T(2,128)(2,1)} %copy.25), calls=%async_computation | async-start | bytes 4096 | tf_op jit(solution)/shard_map/all_to_all | solution.py:41
  29.6 4.9 %copy-start.2 = (f32[1,1,16]{2,1,0:T(1,128)S(1)}, f32[1,1,16]{2,1,0:T(1,128)}, u32[]{:S(2)}) copy-start(f32[1,1,16]{2,1,0:T(1,128)} %param.11) | copy-start | bytes 196
  29.6 46.7 %copy-start.1 = (bf16[1,1,4,128,2048]{4,3,2,1,0:T(8,128)(2,1)S(1)}, bf16[1,1,4,128,2048]{4,3,2,1,0:T(8,128)(2,1)}, u32[]{:S(2)}) copy-start(bf16[1,1,4,128,2048]{4,3,2,1,0:T(8,128)(2,1)} %param.9) | copy-start | bytes 6291460
  29.6 46.7 %all-to-all-start.1 = ((bf16[4,128,3584]{2,1,0:T(8,128)(2,1)}), bf16[4,128,3584]{2,1,0:T(8,128)(2,1)}, u32[]{:S(2)}, u32[]{:S(2)}) async-start(bf16[4,128,3584]{2,1,0:T(8,128)(2,1)} %broadcast_select_fusion), calls=%async_computation.1 | async-start | bytes 7340032 | tf_op jit(solution)/shard_map/all_to_all | solution.py:34
  34.5 130.5 %reduce-scatter.2.cloned.1.call-start = ((), (), s32[]{:S(2)}) async-start(), calls=%async_computation.4 | async-start | bytes 8257536 | tf_op jit(solution)/shard_map/reduce_scatter | solution.py:82
  95.2 7.8 %all-to-all-start.2 = ((f32[4,1,128]{2,1,0:T(1,128)}), f32[4,1,128]{2,1,0:T(1,128)S(1)}, u32[]{:S(2)}, u32[]{:S(2)}) async-start(f32[4,1,128]{2,1,0:T(1,128)} %bitcast.19), calls=%async_computation.3 | async-start | bytes 4096 | tf_op jit(solution)/shard_map/all_to_all | solution.py:95
Sparse Core Ops, SparseCore 0:
  85.0 79.9 reduce-scatter.1
where the time goes:
time: 193 us; the launch traced here: 192 us
  waiting for transfers between devices  86.5 us (45%)
  blocking collectives  30.6 us (16%)
  matrix products  18.8 us (10%)
  between operations  16.2 us (8%)
  local copies, waits for them, and re-layouts  13.7 us (7%)
  other arithmetic  13.5 us (7%)
  starting transfers between devices  13.3 us (7%)
    reduce_scatter x1, waiting for transfers between devices, body(): lax.psum_scatter(term(jnp.int32(0), width // n_replicas * lax.axis_size('...  59.3 us
    all_to_all x1, waiting for transfers between devices, body(): lax.all_to_all(send_rows.reshape(n_ep, local * cap, width), 'ep', split_a...  24.1 us
    pmax x1, blocking collectives, body(): merged = lax.pmax(history, 'ed')[0]  16.3 us
    pmax x1, blocking collectives, body(): peak = lax.pmax(jnp.max(jnp.abs(wgrad), axis=(1, 2)), 'ed')  14.2 us
    dot_general x1, matrix products, body(): jnp.einsum('rd,hd->rh', rows, weight, preferred_element_type=jnp.float32)  10.3 us
    dot_general x1, matrix products, term(): jnp.einsum('rd,rh->dh', rows, weighted, preferred_element_type=jnp.float32)  8.52 us
    all_to_all x1, starting transfers between devices, body(): lax.all_to_all(send_gate.reshape(n_ep, local * cap), 'ep', split_axis=0,...  5.16 us
    all_to_all x1, starting transfers between devices, body(): lax.all_to_all(send_rows.reshape(n_ep, local * cap, width), 'ep', split_a...  4.87 us
  transfers between devices with their start and end apart: 4, of which 3 were waited for; matrix products, arithmetic and copies ran while one was open for 13% of the time, Pallas kernels for 0%

commit v1 on v0

--- a/solution.py
+++ b/solution.py
@@ -1,6 +1,10 @@
+import functools
+
 import jax
 import jax.numpy as jnp
 from jax import lax
+from jax.experimental import pallas as pl
+from jax.experimental.pallas import tpu as pltpu
 from jax.sharding import PartitionSpec as P
 
 
@@ -10,7 +14,7 @@
     return (gate_pre, up_pre, jax.nn.sigmoid(gate_pre))
 
 
-def body(out_grad, routes, gates, pre_acts, down_weight, history):
+def plain(out_grad, routes, gates, pre_acts, down_weight, history):
     tok_rows, top = routes.shape
     width = out_grad.shape[1]
     local = down_weight.shape[0]
@@ -97,6 +101,530 @@
     return (pre_grad, wgrad, new_history, gate_grad)
 
 
+MESH = pl.DeviceIdType.MESH
+LANES = 128
+
+
+def orders(n_z):
+    centre = (n_z - 1) / 2
+    return [
+        sorted(range(n_z), key=lambda j: (-abs(j - z), -abs(j - centre), j)) for z in range(n_z)
+    ]
+
+
+def kernel(
+    n_z,
+    n_ep,
+    cap,
+    routes_ref,
+    gates_ref,
+    hist_ref,
+    tok_hbm,
+    pre_hbm,
+    w_hbm,
+    pg_hbm,
+    wg_hbm,
+    hist_out,
+    gg_out,
+    tok,
+    wv,
+    pre,
+    pgrad,
+    perm,
+    perm_t,
+    outrows,
+    rows,
+    sib,
+    w2,
+    raw,
+    act,
+    rt,
+    acc,
+    recv,
+    zsend,
+    gate_out,
+    gate_in,
+    score_out,
+    score_in,
+    hist_mine,
+    hist_all,
+    amax_mine,
+    amax_all,
+    tok_sem,
+    w_sem,
+    pre_sem,
+    pg_sem,
+    wg_sem,
+    row_ss,
+    row_rs,
+    gate_ss,
+    gate_rs,
+    score_ss,
+    score_rs,
+    sib_ss,
+    sib_rs,
+    w2_ss,
+    w2_rs,
+    z_ss,
+    z_rs,
+    hist_ss,
+    hist_rs,
+    amax_ss,
+    amax_rs,
+):
+    f32, bf16 = jnp.float32, jnp.bfloat16
+    ed, me = lax.axis_index("ed"), lax.axis_index("ep")
+    z, core = ed // 2, ed % 2
+    n_ed = 2 * n_z
+    sibling = z * 2 + 1 - core
+    blk = tok.shape[2]
+    half = blk // 2
+    lane0 = half // LANES * LANES
+    wid = blk - lane0
+    sub = half // 2
+    slots = n_ep * cap
+    ff = act.shape[1]
+    table = orders(n_z)
+
+    def shard_at(i):
+        j = jnp.int32(table[0][i])
+        for at in range(1, n_z):
+            j = jnp.where(z == at, jnp.int32(table[at][i]), j)
+        return j
+
+    shard = [shard_at(i) for i in range(n_z)]
+
+    def columns(i):
+        return pl.ds(pl.multiple_of(shard[i] * blk, LANES), blk)
+
+    tok_in = [
+        pltpu.make_async_copy(tok_hbm.at[:, columns(i)], tok.at[i], tok_sem.at[i])
+        for i in range(n_z)
+    ]
+    w_in = [
+        pltpu.make_async_copy(w_hbm.at[0, :, columns(i)], wv.at[i], w_sem.at[i])
+        for i in range(n_z)
+    ]
+    pre_in = pltpu.make_async_copy(pre_hbm, pre, pre_sem.at[0])
+    tok_in[0].start()
+    pre_in.start()
+    for i in range(1, n_z):
+        tok_in[i].start()
+    for i in range(n_z):
+        w_in[i].start()
+
+    barrier = pltpu.get_barrier_semaphore()
+    for d in range(1, n_ep):
+        pl.semaphore_signal(
+            barrier, inc=1, device_id={"ep": lax.rem(me + d, n_ep)}, device_id_type=MESH
+        )
+    for d in range(1, n_ed):
+        pl.semaphore_signal(
+            barrier, inc=1, device_id={"ed": lax.rem(ed + d, n_ed)}, device_id_type=MESH
+        )
+
+    hist_mine[...] = jnp.zeros_like(hist_mine)
+    hist_mine[0:1, 0 : hist_ref.shape[1]] = hist_ref[...]
+
+    tokens = tok.shape[1]
+    expert = lax.broadcasted_iota(jnp.int32, (tokens, slots), 1) // cap
+    place = lax.broadcasted_iota(jnp.int32, (tokens, slots), 1) % cap
+    hit0 = routes_ref[:, 0:1] == expert
+    hit1 = routes_ref[:, 1:2] == expert
+    hits = jnp.where(hit0, 1.0, 0.0) + jnp.where(hit1, 1.0, 0.0)
+    earlier = lax.broadcasted_iota(jnp.int32, (tokens, tokens), 0) > lax.broadcasted_iota(
+        jnp.int32, (tokens, tokens), 1
+    )
+    slot = jnp.dot(
+        jnp.where(earlier, 1.0, 0.0).astype(bf16), hits.astype(bf16), preferred_element_type=f32
+    )
+    placed = jnp.where(slot == place.astype(f32), hits, 0.0)
+    perm_t[...] = placed
+    g0 = gates_ref[:, 0:1].astype(f32)
+    g1 = gates_ref[:, 1:2].astype(f32)
+    gate_tok = (jnp.where(hit0, g0, 0.0) + jnp.where(hit1, g1, 0.0)).astype(bf16)
+    for e in range(n_ep):
+        own = placed[:, e * cap : (e + 1) * cap].T.astype(bf16)
+        perm[e] = own
+        gate_out[e] = jnp.dot(
+            own, gate_tok[:, e * cap : (e + 1) * cap], preferred_element_type=f32
+        ).astype(bf16)
+    gate_in[me] = gate_out[me]
+
+    pl.semaphore_wait(barrier, n_ep - 1 + n_ed - 1)
+
+    def to_ep(src, dst, ss, rs, d):
+        return pltpu.make_async_remote_copy(
+            src_ref=src, dst_ref=dst, send_sem=ss, recv_sem=rs,
+            device_id={"ep": lax.rem(me + d, n_ep)}, device_id_type=MESH,
+        )
+
+    def to_ed(src, dst, ss, rs, target):
+        return pltpu.make_async_remote_copy(
+            src_ref=src, dst_ref=dst, send_sem=ss, recv_sem=rs,
+            device_id={"ed": target}, device_id_type=MESH,
+        )
+
+    def peer(d):
+        return lax.rem(me + d, n_ep)
+
+    def row_copy(i, d, src):
+        return to_ep(
+            outrows.at[i, peer(d)], rows.at[i, src], row_ss.at[i, d], row_rs.at[i, src], d
+        )
+
+    def gate_copy(d, src):
+        return to_ep(gate_out.at[peer(d)], gate_in.at[src], gate_ss.at[d], gate_rs.at[src], d)
+
+    def score_copy(d, src):
+        return to_ep(score_out.at[peer(d)], score_in.at[src], score_ss.at[d], score_rs.at[src], d)
+
+    def hist_copy(d, src):
+        return to_ed(
+            hist_mine, hist_all.at[src], hist_ss.at[d], hist_rs.at[src], lax.rem(ed + d, n_ed)
+        )
+
+    def amax_copy(d, src):
+        return to_ed(
+            amax_mine, amax_all.at[src], amax_ss.at[d], amax_rs.at[src], lax.rem(ed + d, n_ed)
+        )
+
+    def dispatch(i):
+        tok_in[i].wait()
+
+        @pl.loop(0, n_ep)
+        def _(e):
+            outrows[i, e] = jnp.dot(perm[e], tok[i], preferred_element_type=f32).astype(bf16)
+
+        for d in range(1, n_ep):
+            row_copy(i, d, me).start()
+        rows[i, me] = outrows[i, me]
+
+    for d in range(1, n_ep):
+        gate_copy(d, me).start()
+    dispatch(0)
+    for d in range(1, n_ed):
+        hist_copy(d, ed).start()
+    hist_all[ed] = hist_mine[...]
+
+    tile = 32
+    pre_in.wait()
+    for d in range(1, n_ep):
+        gate_copy(d, peer(d)).wait_recv()
+
+    @pl.loop(0, slots // tile)
+    def _(t):
+        at = pl.ds(pl.multiple_of(t * tile, tile), tile)
+        src, off = t // (cap // tile), t % (cap // tile)
+        off = pl.multiple_of(off * tile, tile)
+        g = pre[src, pl.ds(off, tile), 0:ff].astype(f32)
+        u = pre[src, pl.ds(off, tile), ff:].astype(f32)
+        a = (g * jax.nn.sigmoid(g) * u).astype(bf16)
+        act[at, :] = a
+        gate = gate_in[src, pl.ds(off, tile), 0:1].astype(f32)
+        w2[core, at, :] = (gate * a.astype(f32)).astype(bf16)
+
+    def w2_copy(which):
+        return to_ed(w2.at[which], w2.at[which], w2_ss.at[0], w2_rs.at[0], sibling)
+
+    w2_copy(core).start()
+
+    def sib_copy(i):
+        at = pl.ds(pl.multiple_of(lane0 * (1 - core), LANES), wid)
+        return to_ed(rows.at[i, :, :, at], sib.at[i], sib_ss.at[i], sib_rs.at[i], sibling)
+
+    def z_copy(i, s):
+        right = shard[i] > z
+        target = jnp.where(right, z + 1, z - 1)
+        way = jnp.where(right, 0, 1)
+        return to_ed(
+            zsend.at[i, s], recv.at[way, shard[i], s], z_ss.at[i, s],
+            z_rs.at[way, shard[i], s], target * 2 + core,
+        )
+
+    def z_arrival(way, j, s):
+        return to_ed(
+            zsend.at[0, 0], recv.at[way, j, s], z_ss.at[0, 0], z_rs.at[way, j, s], sibling
+        )
+
+    n_tile = 256
+    etile = 32
+
+    for i in range(n_z):
+        last = i == n_z - 1
+        for d in range(1, n_ep):
+            row_copy(i, d, peer(d)).wait_recv()
+        sib_copy(i).start()
+        if not last:
+            dispatch(i + 1)
+        w_in[i].wait()
+
+        @pl.loop(0, ff // n_tile)
+        def _(n):
+            at = pl.ds(pl.multiple_of(n * n_tile, n_tile), n_tile)
+            got = lax.dot_general(
+                rows[i].reshape(slots, blk), wv[i, at, :], (((1,), (1,)), ((), ())),
+                preferred_element_type=f32,
+            )
+            if i == 0:
+                raw[:, at] = got
+            else:
+                raw[:, at] += got
+
+        if i == 0:
+            w2_copy(1 - core).wait_recv()
+        sib_copy(i).wait_recv()
+        mine = pl.ds(pl.multiple_of(lane0 * core, LANES), wid)
+        rt[:, pl.ds(pl.multiple_of(core * slots, LANES), slots)] = (
+            rows[i, :, :, mine].reshape(slots, wid).T
+        )
+        rt[:, pl.ds(pl.multiple_of((1 - core) * slots, LANES), slots)] = (
+            sib[i].reshape(slots, wid).T
+        )
+        start = pl.multiple_of((half - lane0) * core, 16)
+
+        @pl.loop(0, ff // n_tile)
+        def _(n):
+            at = pl.ds(pl.multiple_of(n * n_tile, n_tile), n_tile)
+            acc[:, at] = jnp.dot(
+                rt[pl.ds(start, half), :],
+                w2[:, :, at].reshape(2 * slots, n_tile),
+                preferred_element_type=f32,
+            )
+
+        if last:
+            break
+        right = shard[i] > z
+        way = jnp.where(right, 0, 1)
+        fed = jnp.where(right, z > 0, z < n_z - 1)
+        for s in range(2):
+
+            @pl.when(fed)
+            def _():
+                z_arrival(way, shard[i], s).wait_recv()
+
+                @pl.loop(0, sub // etile)
+                def _(t):
+                    off = pl.multiple_of(t * etile, etile)
+                    own = acc[pl.ds(s * sub + off, etile), :]
+                    came = recv[way, shard[i], s, pl.ds(off, etile), :].astype(f32)
+                    zsend[i, s, pl.ds(off, etile), :] = (own + came).astype(bf16)
+
+            @pl.when(jnp.logical_not(fed))
+            def _():
+                @pl.loop(0, sub // etile)
+                def _(t):
+                    off = pl.multiple_of(t * etile, etile)
+                    own = acc[pl.ds(s * sub + off, etile), :]
+                    zsend[i, s, pl.ds(off, etile), :] = own.astype(bf16)
+
+            z_copy(i, s).start()
+
+    @pl.loop(0, slots // tile)
+    def _(t):
+        at = pl.ds(pl.multiple_of(t * tile, tile), tile)
+        src, off = t // (cap // tile), t % (cap // tile)
+        off = pl.multiple_of(off * tile, tile)
+        g = pre[src, pl.ds(off, tile), 0:ff].astype(f32)
+        u = pre[src, pl.ds(off, tile), ff:].astype(f32)
+        sigma = jax.nn.sigmoid(g)
+        r = raw[at, :]
+        total = jnp.sum(act[at, :].astype(f32) * r, axis=1, keepdims=True)
+        score_out[src, pl.ds(off, tile), :] = jnp.broadcast_to(total, (tile, LANES))
+        gr = gate_in[src, pl.ds(off, tile), 0:1].astype(f32) * r
+        pgrad[src, pl.ds(off, tile), 0:ff] = (gr * u * sigma * (1.0 + g * (1.0 - sigma))).astype(
+            bf16
+        )
+        pgrad[src, pl.ds(off, tile), ff:] = (gr * g * sigma).astype(bf16)
+
+    pg_copy = pltpu.make_async_copy(pgrad, pg_hbm, pg_sem.at[0])
+    pg_copy.start()
+    for d in range(1, n_ep):
+        score_copy(d, me).start()
+    score_in[me] = score_out[me]
+
+    for d in range(1, n_ed):
+        hist_copy(d, lax.rem(ed + d, n_ed)).wait_recv()
+    merged = jnp.max(hist_all[...], axis=0)
+    ref_amax = jnp.max(merged)
+    scale = 1.0 / jnp.full((1, 1), ref_amax, f32)
+
+    for d in range(1, n_ep):
+        score_copy(d, peer(d)).wait_recv()
+    diagonal = lax.broadcasted_iota(jnp.int32, (cap, LANES), 0) == lax.broadcasted_iota(
+        jnp.int32, (cap, LANES), 1
+    )
+    value0 = jnp.zeros((tokens, 1), f32)
+    value1 = jnp.zeros((tokens, 1), f32)
+    for e in range(n_ep):
+        line = jnp.sum(jnp.where(diagonal, score_in[e], 0.0), axis=0, keepdims=True)
+        found = jnp.sum(perm_t[:, e * cap : (e + 1) * cap] * line, axis=1, keepdims=True)
+        value0 = value0 + jnp.where(routes_ref[:, 0:1] == e, found, 0.0)
+        value1 = value1 + jnp.where(routes_ref[:, 1:2] == e, found, 0.0)
+    pair = lax.broadcasted_iota(jnp.int32, (tokens, 2), 1)
+    gg_out[...] = jnp.where(pair == 0, value0, value1)
+
+    own_shard = shard[n_z - 1]
+    amax_mine[...] = jnp.zeros_like(amax_mine)
+
+    wg_copy = []
+    for s in range(2):
+        for way in range(2):
+            there = z > 0 if way == 0 else z < n_z - 1
+
+            @pl.when(there)
+            def _():
+                z_arrival(way, own_shard, s).wait_recv()
+
+                @pl.loop(0, sub // etile)
+                def _(t):
+                    off = pl.multiple_of(t * etile, etile)
+                    at = pl.ds(s * sub + off, etile)
+                    acc[at, :] += recv[way, own_shard, s, pl.ds(off, etile), :].astype(f32)
+
+        @pl.loop(0, sub // etile)
+        def _(t):
+            at = pl.ds(pl.multiple_of(s * sub + t * etile, etile), etile)
+            value = acc[at, :] * scale
+            acc[at, :] = value
+            large = jnp.max(jnp.abs(value).reshape(etile // 8, 8, ff // LANES, LANES), axis=(0, 2))
+            amax_mine[...] = jnp.maximum(amax_mine[...], large)
+
+        copy = pltpu.make_async_copy(
+            acc.at[pl.ds(s * sub, sub), :], wg_hbm.at[0, pl.ds(s * sub, sub), :], wg_sem.at[s]
+        )
+        copy.start()
+        wg_copy.append(copy)
+
+    for d in range(1, n_ed):
+        amax_copy(d, ed).start()
+    amax_all[ed] = amax_mine[...]
+    for d in range(1, n_ed):
+        amax_copy(d, lax.rem(ed + d, n_ed)).wait_recv()
+    peak = jnp.max(amax_all[...]) * ref_amax
+    width = hist_ref.shape[1]
+    moved = pltpu.roll(merged, LANES - 1, 1)
+    lane = lax.broadcasted_iota(jnp.int32, merged.shape, 1)
+    hist_out[...] = jnp.where(lane == width - 1, peak, moved)[0:1, 0:width]
+
+    for d in range(1, n_ep):
+        for i in range(n_z):
+            row_copy(i, d, me).wait_send()
+        gate_copy(d, me).wait_send()
+        score_copy(d, me).wait_send()
+    for d in range(1, n_ed):
+        hist_copy(d, ed).wait_send()
+        amax_copy(d, ed).wait_send()
+    w2_copy(core).wait_send()
+    for i in range(n_z):
+        sib_copy(i).wait_send()
+    for i in range(n_z - 1):
+        for s in range(2):
+            z_copy(i, s).wait_send()
+    pg_copy.wait()
+    for copy in wg_copy:
+        copy.wait()
+
+
+def fused(out_grad, routes, gates, pre_acts, down_weight, history):
+    f32, bf16, dma = jnp.float32, jnp.bfloat16, pltpu.SemaphoreType.DMA
+    tokens, width = out_grad.shape
+    ff = down_weight.shape[1]
+    n_src, cap = pre_acts.shape[2], pre_acts.shape[3]
+    n_ep, n_ed = lax.axis_size("ep"), lax.axis_size("ed")
+    n_z = n_ed // 2
+    hist = history.shape[2]
+    blk = width // n_z
+    half = blk // 2
+    wid = blk - half // LANES * LANES
+    slots = n_ep * cap
+    vmem, anywhere = pl.BlockSpec(memory_space=pltpu.VMEM), pl.BlockSpec(memory_space=pl.ANY)
+    pre_grad, wgrad, new_history, gate_grad = pl.pallas_call(
+        functools.partial(kernel, n_z, n_ep, cap),
+        out_shape=(
+            jax.ShapeDtypeStruct((n_src, cap, 2 * ff), bf16),
+            jax.ShapeDtypeStruct((1, half, ff), f32),
+            jax.ShapeDtypeStruct((1, hist), f32),
+            jax.ShapeDtypeStruct((tokens, 2), f32),
+        ),
+        in_specs=[vmem, vmem, vmem, anywhere, anywhere, anywhere],
+        out_specs=(anywhere, anywhere, vmem, vmem),
+        scratch_shapes=[
+            pltpu.VMEM((n_z, tokens, blk), bf16),
+            pltpu.VMEM((n_z, ff, blk), bf16),
+            pltpu.VMEM((n_src, cap, 2 * ff), bf16),
+            pltpu.VMEM((n_src, cap, 2 * ff), bf16),
+            pltpu.VMEM((n_ep, cap, tokens), bf16),
+            pltpu.VMEM((tokens, slots), f32),
+            pltpu.VMEM((n_z, n_ep, cap, blk), bf16),
+            pltpu.VMEM((n_z, n_ep, cap, blk), bf16),
+            pltpu.VMEM((n_z, n_ep, cap, wid), bf16),
+            pltpu.VMEM((2, slots, ff), bf16),
+            pltpu.VMEM((slots, ff), f32),
+            pltpu.VMEM((slots, ff), bf16),
+            pltpu.VMEM((wid, 2 * slots), bf16),
+            pltpu.VMEM((half, ff), f32),
+            pltpu.VMEM((2, n_z, 2, half // 2, ff), bf16),
+            pltpu.VMEM((n_z - 1, 2, half // 2, ff), bf16),
+            pltpu.VMEM((n_ep, cap, LANES), bf16),
+            pltpu.VMEM((n_ep, cap, LANES), bf16),
+            pltpu.VMEM((n_ep, cap, LANES), f32),
+            pltpu.VMEM((n_ep, cap, LANES), f32),
+            pltpu.VMEM((8, LANES), f32),
+            pltpu.VMEM((n_ed, 8, LANES), f32),
+            pltpu.VMEM((8, LANES), f32),
+            pltpu.VMEM((n_ed, 8, LANES), f32),
+            dma((n_z,)),
+            dma((n_z,)),
+            dma((1,)),
+            dma((1,)),
+            dma((2,)),
+            dma((n_z, n_ep)),
+            dma((n_z, n_ep)),
+            dma((n_ep,)),
+            dma((n_ep,)),
+            dma((n_ep,)),
+            dma((n_ep,)),
+            dma((n_z,)),
+            dma((n_z,)),
+            dma((1,)),
+            dma((1,)),
+            dma((n_z, 2)),
+            dma((2, n_z, 2)),
+            dma((n_ed,)),
+            dma((n_ed,)),
+            dma((n_ed,)),
+            dma((n_ed,)),
+        ],
+        compiler_params=pltpu.CompilerParams(
+            collective_id=0, has_side_effects=True, vmem_limit_bytes=56 * 1024 * 1024
+        ),
+        cost_estimate=pl.CostEstimate(
+            flops=4 * slots * width * ff, bytes_accessed=16 * 1024 * 1024, transcendentals=slots * ff
+        ),
+    )(
+        routes, gates, history[0], out_grad, pre_acts[0, 0], down_weight
+    )
+    return pre_grad[None, None], wgrad, new_history, gate_grad
+
+
+def body(out_grad, routes, gates, pre_acts, down_weight, history):
+    tokens, width = out_grad.shape
+    cap = pre_acts.shape[3]
+    n_ed = lax.axis_size("ed")
+    fits = (
+        n_ed % 2 == 0
+        and n_ed > 2
+        and cap == LANES
+        and tokens == LANES
+        and down_weight.shape[0] == 1
+        and width % (n_ed // 2 * LANES) == 0
+        and width // n_ed % 64 == 0
+    )
+    run = fused if fits else plain
+    return run(out_grad, routes, gates, pre_acts, down_weight, history)
+
+
 def solution(mesh):
     placed = (
         P(("ed", "ep"), None),

time: 193 us -> 101 us (0.52)
  Pallas kernels: 0 us -> 91 us
  waiting for transfers between devices: 86.5 us -> 0 us
  blocking collectives: 30.6 us -> 0 us
  matrix products: 18.8 us -> 0 us
  between operations: 16.2 us -> 0.64 us
  other arithmetic: 13.5 us -> 0 us
  starting transfers between devices: 13.3 us -> 0 us
  local copies, waits for them, and re-layouts: 13.7 us -> 9.31 us
    pallas_call x0 -> x1, Pallas kernels: none -> 91 us  [fused(): pl.pallas_call(functools.partial(kernel, n_z, n_ep, cap), out_shape=(jax....]
    reduce_scatter x1 -> x0, waiting for transfers between devices: 59.3 us -> none  [body(): lax.psum_scatter(term(jnp.int32(0), width // n_replicas * lax.axis_size('...]
    pmax x2 -> x0, blocking collectives: 30.6 us -> none  [the longest x1 16.3 us: body(): merged = lax.pmax(history, 'ed')[0]]
    all_to_all x3 -> x0, waiting for transfers between devices: 27.2 us -> none  [the longest x1 24.1 us: body(): lax.all_to_all(send_rows.reshape(n_ep, local * cap, width), 'ep', split_a...]
    dot_general x2 -> x0, matrix products: 18.8 us -> none  [the longest x1 10.3 us: body(): jnp.einsum('rd,hd->rh', rows, weight, preferred_element_type=jnp.float32)]
    all_to_all x3 -> x0, starting transfers between devices: 13.3 us -> none  [the longest x1 5.16 us: body(): lax.all_to_all(send_gate.reshape(n_ep, local * cap), 'ep', split_axis=0,...]
    unnamed x9 -> x10, local copies, waits for them, and re-layouts: 2.23 us -> 9.31 us
    gather x2 -> x0, local copies, waits for them, and re-layouts: 6.16 us -> none  [the longest x1 4.22 us: body(): picked = out_grad[jnp.maximum(table - 1, 0)]]
  transfers between devices with their start and end apart: 4 -> 0, of which waited for: 3 -> 0; matrix products, arithmetic and copies ran while one was open for 13% -> 0% of each run, Pallas kernels for 0% -> 0%
where the time goes in v1:
time: 101 us
  Pallas kernels  91 us (90%)
  local copies, waits for them, and re-layouts  9.31 us (9%)
    pallas_call x1, Pallas kernels, fused(): pl.pallas_call(functools.partial(kernel, n_z, n_ep, cap), out_shape=(jax....  91 us
    unnamed x10, local copies, waits for them, and re-layouts  9.31 us

profile of v1, /device:TPU:0, one launch (start us, length us, event | category | flops | bytes accessed | tf_op | source)
XLA Modules:
  0.0 100.9 jit_solution(16455200461189338219)
XLA Ops:
  0.6 1.4 %copy.11.gates_ref = bf16[128,2]{1,0:T(8,128)(2,1)} copy(bf16[128,2]{0,1:T(2,128)(2,1)} %param.8) | data formatting | bytes 1024 | tf_op args[2]
  2.0 1.4 %copy.10.routes_ref = s32[128,2]{1,0:T(8,128)} copy(s32[128,2]{0,1:T(2,128)} %param.7) | data formatting | bytes 2048 | tf_op args[1]
  3.4 91.0 %shard_map.93 = (bf16[4,128,2048]{2,1,0:T(8,128)(2,1)}, f32[1,448,1024]{2,1,0:T(8,128)}, f32[1,16]{1,0:T(1,128)}, f32[128,2]{1,0:T(8,128)}) custom-call(s32[128,2]{1,0:T(8,128)} %copy.10.routes_ref, bf16[128,2]{1,0:T(8,128)(2,1)} %copy.11.gates_ref, f32[1,16]{1,0:T(1,128)} %bitcast.5, bf16[128,3584]{1,0:T(8,128)(2,1)} %tok_hbm.1, ...), custom_call_target="tpu_custom_call" | custom-call | flops 7516192768 | bytes 16777216 | tf_op jit(solution)/shard_map/pallas_call | solution.py:542
  94.4 1.5 %copy.12 = f32[128,2]{0,1:T(2,128)} copy(f32[128,2]{1,0:T(8,128)} %get-tuple-element.15) | data formatting | bytes 2048
  95.9 0.0 copy-start
  95.9 3.3 %copy.16 = bf16[1,1,4,128,2048]{4,3,2,1,0:T(8,128)(2,1)} copy(bf16[1,1,4,128,2048]{4,3,2,1,0:T(8,128)(2,1)} %bitcast.3) | data formatting | bytes 4194304
  99.2 0.0 copy-done
  99.2 0.0 copy-start.1
  99.2 1.2 %copy.17 = f32[1,448,1024]{2,1,0:T(8,128)} copy(f32[1,448,1024]{2,1,0:T(8,128)S(1)} %copy-done) | data formatting | bytes 3670016
  100.4 0.0 copy-done.1
  100.4 0.5 copy.18
Async XLA Ops:
  95.9 3.3 %copy-start = (f32[1,448,1024]{2,1,0:T(8,128)S(1)}, f32[1,448,1024]{2,1,0:T(8,128)}, u32[]{:S(2)}) copy-start(f32[1,448,1024]{2,1,0:T(8,128)} %get-tuple-element.21) | copy-start | bytes 5505028
  99.2 1.2 %copy-start.1 = (f32[1,16]{1,0:T(1,128)S(1)}, f32[1,16]{1,0:T(1,128)}, u32[]{:S(2)}) copy-start(f32[1,16]{1,0:T(1,128)} %get-tuple-element.22) | copy-start | bytes 196

commit v2 on v1

--- a/solution.py
+++ b/solution.py
@@ -112,6 +112,12 @@
     ]
 
 
+def split_half(half):
+    big = -(-half // (2 * LANES)) * LANES
+    small = half - big
+    return big, small, -(-small // LANES) * LANES
+
+
 def kernel(
     n_z,
     n_ep,
@@ -122,14 +128,13 @@
     tok_hbm,
     pre_hbm,
     w_hbm,
-    pg_hbm,
-    wg_hbm,
+    pgrad,
+    wg_out,
     hist_out,
     gg_out,
     tok,
     wv,
     pre,
-    pgrad,
     perm,
     perm_t,
     outrows,
@@ -153,8 +158,6 @@
     tok_sem,
     w_sem,
     pre_sem,
-    pg_sem,
-    wg_sem,
     row_ss,
     row_rs,
     gate_ss,
@@ -179,9 +182,8 @@
     sibling = z * 2 + 1 - core
     blk = tok.shape[2]
     half = blk // 2
-    lane0 = half // LANES * LANES
-    wid = blk - lane0
-    sub = half // 2
+    big, small, win = split_half(half)
+    rest = blk - 2 * big
     slots = n_ep * cap
     ff = act.shape[1]
     table = orders(n_z)
@@ -194,24 +196,43 @@
 
     shard = [shard_at(i) for i in range(n_z)]
 
-    def columns(i):
-        return pl.ds(pl.multiple_of(shard[i] * blk, LANES), blk)
+    pieces = ((0, 0, big), (blk - big, big, big), (big, 2 * big, rest))
+
+    def columns(i, begin, count):
+        return pl.ds(pl.multiple_of(shard[i] * blk + begin, LANES), count)
 
     tok_in = [
-        pltpu.make_async_copy(tok_hbm.at[:, columns(i)], tok.at[i], tok_sem.at[i])
+        [
+            pltpu.make_async_copy(
+                tok_hbm.at[:, columns(i, begin, count)],
+                tok.at[i, :, pl.ds(to, count)],
+                tok_sem.at[i, p],
+            )
+            for p, (begin, to, count) in enumerate(pieces)
+        ]
         for i in range(n_z)
     ]
     w_in = [
-        pltpu.make_async_copy(w_hbm.at[0, :, columns(i)], wv.at[i], w_sem.at[i])
+        [
+            pltpu.make_async_copy(
+                w_hbm.at[0, :, columns(i, begin, count)],
+                wv.at[i, :, pl.ds(to, count)],
+                w_sem.at[i, p],
+            )
+            for p, (begin, to, count) in enumerate(pieces)
+        ]
         for i in range(n_z)
     ]
     pre_in = pltpu.make_async_copy(pre_hbm, pre, pre_sem.at[0])
-    tok_in[0].start()
+    for copy in tok_in[0]:
+        copy.start()
     pre_in.start()
     for i in range(1, n_z):
-        tok_in[i].start()
+        for copy in tok_in[i]:
+            copy.start()
     for i in range(n_z):
-        w_in[i].start()
+        for copy in w_in[i]:
+            copy.start()
 
     barrier = pltpu.get_barrier_semaphore()
     for d in range(1, n_ep):
@@ -227,30 +248,37 @@
     hist_mine[0:1, 0 : hist_ref.shape[1]] = hist_ref[...]
 
     tokens = tok.shape[1]
-    expert = lax.broadcasted_iota(jnp.int32, (tokens, slots), 1) // cap
-    place = lax.broadcasted_iota(jnp.int32, (tokens, slots), 1) % cap
-    hit0 = routes_ref[:, 0:1] == expert
-    hit1 = routes_ref[:, 1:2] == expert
-    hits = jnp.where(hit0, 1.0, 0.0) + jnp.where(hit1, 1.0, 0.0)
-    earlier = lax.broadcasted_iota(jnp.int32, (tokens, tokens), 0) > lax.broadcasted_iota(
+    first, second = routes_ref[0:1, :], routes_ref[1:2, :]
+    gate0, gate1 = gates_ref[0:1, :].astype(f32), gates_ref[1:2, :].astype(f32)
+    expert = lax.broadcasted_iota(jnp.int32, (16, tokens), 0)
+    hits = jnp.where(first == expert, 1.0, 0.0) + jnp.where(second == expert, 1.0, 0.0)
+    earlier = lax.broadcasted_iota(jnp.int32, (tokens, tokens), 0) < lax.broadcasted_iota(
         jnp.int32, (tokens, tokens), 1
     )
     slot = jnp.dot(
-        jnp.where(earlier, 1.0, 0.0).astype(bf16), hits.astype(bf16), preferred_element_type=f32
-    )
-    placed = jnp.where(slot == place.astype(f32), hits, 0.0)
-    perm_t[...] = placed
-    g0 = gates_ref[:, 0:1].astype(f32)
-    g1 = gates_ref[:, 1:2].astype(f32)
-    gate_tok = (jnp.where(hit0, g0, 0.0) + jnp.where(hit1, g1, 0.0)).astype(bf16)
+        hits.astype(bf16), jnp.where(earlier, 1.0, 0.0).astype(bf16), preferred_element_type=f32
+    )
+    place = lax.broadcasted_iota(jnp.int32, (cap, tokens), 0).astype(f32)
     for e in range(n_ep):
-        own = placed[:, e * cap : (e + 1) * cap].T.astype(bf16)
-        perm[e] = own
-        gate_out[e] = jnp.dot(
-            own, gate_tok[:, e * cap : (e + 1) * cap], preferred_element_type=f32
-        ).astype(bf16)
+        own = jnp.where(slot[e : e + 1, :] == place, hits[e : e + 1, :], 0.0)
+        perm_t[e] = own
+        perm[e] = own.astype(bf16)
+        gate = jnp.where(first == e, gate0, 0.0) + jnp.where(second == e, gate1, 0.0)
+        column = jnp.sum(own * gate, axis=1, keepdims=True)
+        gate_out[e] = jnp.broadcast_to(column, (cap, LANES)).astype(bf16)
     gate_in[me] = gate_out[me]
 
+    def place_rows(i):
+        for copy in tok_in[i]:
+            copy.wait()
+
+        @pl.loop(0, n_ep)
+        def _(e):
+            outrows[i, e] = jnp.dot(perm[e], tok[i], preferred_element_type=f32).astype(bf16)
+
+        rows[i, me] = outrows[i, me]
+
+    place_rows(0)
     pl.semaphore_wait(barrier, n_ep - 1 + n_ed - 1)
 
     def to_ep(src, dst, ss, rs, d):
@@ -268,9 +296,12 @@
     def peer(d):
         return lax.rem(me + d, n_ep)
 
-    def row_copy(i, d, src):
+    spans = (pl.ds(0, 2 * big), pl.ds(2 * big, rest))
+
+    def row_copy(i, a, d, src):
         return to_ep(
-            outrows.at[i, peer(d)], rows.at[i, src], row_ss.at[i, d], row_rs.at[i, src], d
+            outrows.at[i, peer(d), :, spans[a]], rows.at[i, src, :, spans[a]],
+            row_ss.at[i, a, d], row_rs.at[i, a, src], d,
         )
 
     def gate_copy(d, src):
@@ -289,23 +320,26 @@
             amax_mine, amax_all.at[src], amax_ss.at[d], amax_rs.at[src], lax.rem(ed + d, n_ed)
         )
 
-    def dispatch(i):
-        tok_in[i].wait()
-
-        @pl.loop(0, n_ep)
-        def _(e):
-            outrows[i, e] = jnp.dot(perm[e], tok[i], preferred_element_type=f32).astype(bf16)
-
+    def dispatch(i, a):
         for d in range(1, n_ep):
-            row_copy(i, d, me).start()
-        rows[i, me] = outrows[i, me]
-
+            row_copy(i, a, d, me).start()
+
+    dispatch(0, 0)
     for d in range(1, n_ep):
         gate_copy(d, me).start()
-    dispatch(0)
     for d in range(1, n_ed):
         hist_copy(d, ed).start()
     hist_all[ed] = hist_mine[...]
+
+    @pl.when(z == 0)
+    def _():
+        recv[0, z] = jnp.zeros(recv.shape[2:], bf16)
+
+    @pl.when(z == n_z - 1)
+    def _():
+        recv[1, z] = jnp.zeros(recv.shape[2:], bf16)
+
+    place_rows(1)
 
     tile = 32
     pre_in.wait()
@@ -329,35 +363,97 @@
 
     w2_copy(core).start()
 
-    def sib_copy(i):
-        at = pl.ds(pl.multiple_of(lane0 * (1 - core), LANES), wid)
-        return to_ed(rows.at[i, :, :, at], sib.at[i], sib_ss.at[i], sib_rs.at[i], sibling)
+    def window(a, which):
+        if a == 0:
+            return pl.ds(pl.multiple_of(which * big, LANES), big)
+        return pl.ds(pl.multiple_of(2 * big + which * (rest - win), LANES), win)
+
+    heights = (big, small)
+    starts = (0, big)
+    wide = (big, win)
+
+    def sib_copy(i, a):
+        return to_ed(
+            rows.at[i, :, :, window(a, 1 - core)], sib.at[i, a, :, :, pl.ds(0, wide[a])],
+            sib_ss.at[i, a], sib_rs.at[i, a], sibling,
+        )
 
     def z_copy(i, s):
         right = shard[i] > z
         target = jnp.where(right, z + 1, z - 1)
         way = jnp.where(right, 0, 1)
+        at = pl.ds(starts[s], heights[s])
         return to_ed(
-            zsend.at[i, s], recv.at[way, shard[i], s], z_ss.at[i, s],
+            zsend.at[i, at], recv.at[way, shard[i], at], z_ss.at[i, s],
             z_rs.at[way, shard[i], s], target * 2 + core,
         )
 
     def z_arrival(way, j, s):
+        at = pl.ds(starts[s], heights[s])
         return to_ed(
-            zsend.at[0, 0], recv.at[way, j, s], z_ss.at[0, 0], z_rs.at[way, j, s], sibling
+            zsend.at[0, at], recv.at[way, j, at], z_ss.at[0, 0], z_rs.at[way, j, s], sibling
         )
 
     n_tile = 256
     etile = 32
 
+    def part(i, a):
+        sib_copy(i, a).start()
+        rt[0 : wide[a], pl.ds(pl.multiple_of(core * slots, LANES), slots)] = (
+            rows[i, :, :, window(a, core)].reshape(slots, wide[a]).T
+        )
+        if i == 0 and a == 0:
+            w2_copy(1 - core).wait_recv()
+        sib_copy(i, a).wait_recv()
+        rt[0 : wide[a], pl.ds(pl.multiple_of((1 - core) * slots, LANES), slots)] = (
+            sib[i, a, :, :, 0 : wide[a]].reshape(slots, wide[a]).T
+        )
+        skip = 0 if a == 0 else pl.multiple_of((small - (rest - win)) * core, 16)
+
+        @pl.loop(0, ff // n_tile)
+        def _(n):
+            at = pl.ds(pl.multiple_of(n * n_tile, n_tile), n_tile)
+            acc[starts[a] : starts[a] + heights[a], at] = jnp.dot(
+                rt[pl.ds(skip, heights[a]), :],
+                w2[:, :, at].reshape(2 * slots, n_tile),
+                preferred_element_type=f32,
+            )
+
+    def send_on(i, s, came_by):
+        @pl.loop(0, heights[s] // etile)
+        def _(t):
+            at = pl.ds(pl.multiple_of(starts[s] + t * etile, etile), etile)
+            value = acc[at, :]
+            if came_by is not None:
+                value = value + recv[came_by, shard[i], at, :].astype(f32)
+            zsend[i, at, :] = value.astype(bf16)
+
+        if i > 0:
+            z_copy(i - 1, s).wait_send()
+        z_copy(i, s).start()
+
     for i in range(n_z):
         last = i == n_z - 1
-        for d in range(1, n_ep):
-            row_copy(i, d, peer(d)).wait_recv()
-        sib_copy(i).start()
-        if not last:
-            dispatch(i + 1)
-        w_in[i].wait()
+        right = shard[i] > z
+        way = jnp.where(right, 0, 1)
+        fed = jnp.where(right, z > 0, z < n_z - 1)
+        for a in range(2):
+            for d in range(1, n_ep):
+                row_copy(i, a, d, peer(d)).wait_recv()
+            if i == 0 and a == 0:
+                dispatch(0, 1)
+            if not last and a == 1:
+                dispatch(i + 1, 0)
+                dispatch(i + 1, 1)
+            part(i, a)
+            if not last:
+
+                @pl.when(jnp.logical_not(fed))
+                def _():
+                    send_on(i, a, None)
+
+        for copy in w_in[i]:
+            copy.wait()
 
         @pl.loop(0, ff // n_tile)
         def _(n):
@@ -371,54 +467,16 @@
             else:
                 raw[:, at] += got
 
-        if i == 0:
-            w2_copy(1 - core).wait_recv()
-        sib_copy(i).wait_recv()
-        mine = pl.ds(pl.multiple_of(lane0 * core, LANES), wid)
-        rt[:, pl.ds(pl.multiple_of(core * slots, LANES), slots)] = (
-            rows[i, :, :, mine].reshape(slots, wid).T
-        )
-        rt[:, pl.ds(pl.multiple_of((1 - core) * slots, LANES), slots)] = (
-            sib[i].reshape(slots, wid).T
-        )
-        start = pl.multiple_of((half - lane0) * core, 16)
-
-        @pl.loop(0, ff // n_tile)
-        def _(n):
-            at = pl.ds(pl.multiple_of(n * n_tile, n_tile), n_tile)
-            acc[:, at] = jnp.dot(
-                rt[pl.ds(start, half), :],
-                w2[:, :, at].reshape(2 * slots, n_tile),
-                preferred_element_type=f32,
-            )
-
+        if i + 2 < n_z:
+            place_rows(i + 2)
         if last:
             break
-        right = shard[i] > z
-        way = jnp.where(right, 0, 1)
-        fed = jnp.where(right, z > 0, z < n_z - 1)
-        for s in range(2):
-
-            @pl.when(fed)
-            def _():
+
+        @pl.when(fed)
+        def _():
+            for s in range(2):
                 z_arrival(way, shard[i], s).wait_recv()
-
-                @pl.loop(0, sub // etile)
-                def _(t):
-                    off = pl.multiple_of(t * etile, etile)
-                    own = acc[pl.ds(s * sub + off, etile), :]
-                    came = recv[way, shard[i], s, pl.ds(off, etile), :].astype(f32)
-                    zsend[i, s, pl.ds(off, etile), :] = (own + came).astype(bf16)
-
-            @pl.when(jnp.logical_not(fed))
-            def _():
-                @pl.loop(0, sub // etile)
-                def _(t):
-                    off = pl.multiple_of(t * etile, etile)
-                    own = acc[pl.ds(s * sub + off, etile), :]
-                    zsend[i, s, pl.ds(off, etile), :] = own.astype(bf16)
-
-            z_copy(i, s).start()
+                send_on(i, s, way)
 
     @pl.loop(0, slots // tile)
     def _(t):
@@ -437,8 +495,6 @@
         )
         pgrad[src, pl.ds(off, tile), ff:] = (gr * g * sigma).astype(bf16)
 
-    pg_copy = pltpu.make_async_copy(pgrad, pg_hbm, pg_sem.at[0])
-    pg_copy.start()
     for d in range(1, n_ep):
         score_copy(d, me).start()
     score_in[me] = score_out[me]
@@ -451,50 +507,36 @@
 
     for d in range(1, n_ep):
         score_copy(d, peer(d)).wait_recv()
-    diagonal = lax.broadcasted_iota(jnp.int32, (cap, LANES), 0) == lax.broadcasted_iota(
-        jnp.int32, (cap, LANES), 1
-    )
-    value0 = jnp.zeros((tokens, 1), f32)
-    value1 = jnp.zeros((tokens, 1), f32)
+    value0 = jnp.zeros((1, tokens), f32)
+    value1 = jnp.zeros((1, tokens), f32)
     for e in range(n_ep):
-        line = jnp.sum(jnp.where(diagonal, score_in[e], 0.0), axis=0, keepdims=True)
-        found = jnp.sum(perm_t[:, e * cap : (e + 1) * cap] * line, axis=1, keepdims=True)
-        value0 = value0 + jnp.where(routes_ref[:, 0:1] == e, found, 0.0)
-        value1 = value1 + jnp.where(routes_ref[:, 1:2] == e, found, 0.0)
-    pair = lax.broadcasted_iota(jnp.int32, (tokens, 2), 1)
-    gg_out[...] = jnp.where(pair == 0, value0, value1)
-
-    own_shard = shard[n_z - 1]
+        found = jnp.sum(perm_t[e] * score_in[e], axis=0, keepdims=True)
+        value0 = value0 + jnp.where(first == e, found, 0.0)
+        value1 = value1 + jnp.where(second == e, found, 0.0)
+    gg_out[0:1, :] = value0
+    gg_out[1:2, :] = value1
+
     amax_mine[...] = jnp.zeros_like(amax_mine)
-
-    wg_copy = []
     for s in range(2):
-        for way in range(2):
-            there = z > 0 if way == 0 else z < n_z - 1
-
-            @pl.when(there)
-            def _():
-                z_arrival(way, own_shard, s).wait_recv()
-
-                @pl.loop(0, sub // etile)
-                def _(t):
-                    off = pl.multiple_of(t * etile, etile)
-                    at = pl.ds(s * sub + off, etile)
-                    acc[at, :] += recv[way, own_shard, s, pl.ds(off, etile), :].astype(f32)
-
-        @pl.loop(0, sub // etile)
+
+        @pl.when(z > 0)
+        def _():
+            z_arrival(0, z, s).wait_recv()
+
+        @pl.when(z < n_z - 1)
+        def _():
+            z_arrival(1, z, s).wait_recv()
+
+        base = core * small if s == 0 else (1 - core) * big
+
+        @pl.loop(0, heights[s] // etile)
         def _(t):
-            at = pl.ds(pl.multiple_of(s * sub + t * etile, etile), etile)
-            value = acc[at, :] * scale
-            acc[at, :] = value
+            at = pl.ds(pl.multiple_of(starts[s] + t * etile, etile), etile)
+            came = recv[0, z, at, :].astype(f32) + recv[1, z, at, :].astype(f32)
+            value = (acc[at, :] + came) * scale
+            wg_out[0, pl.ds(pl.multiple_of(base + t * etile, etile), etile), :] = value
             large = jnp.max(jnp.abs(value).reshape(etile // 8, 8, ff // LANES, LANES), axis=(0, 2))
             amax_mine[...] = jnp.maximum(amax_mine[...], large)
-
-        copy = pltpu.make_async_copy(
-            acc.at[pl.ds(s * sub, sub), :], wg_hbm.at[0, pl.ds(s * sub, sub), :], wg_sem.at[s]
-        )
-        copy.start()
-        wg_copy.append(copy)
 
     for d in range(1, n_ed):
         amax_copy(d, ed).start()
@@ -509,7 +551,8 @@
 
     for d in range(1, n_ep):
         for i in range(n_z):
-            row_copy(i, d, me).wait_send()
+            for a in range(2):
+                row_copy(i, a, d, me).wait_send()
         gate_copy(d, me).wait_send()
         score_copy(d, me).wait_send()
     for d in range(1, n_ed):
@@ -517,13 +560,10 @@
         amax_copy(d, ed).wait_send()
     w2_copy(core).wait_send()
     for i in range(n_z):
-        sib_copy(i).wait_send()
-    for i in range(n_z - 1):
-        for s in range(2):
-            z_copy(i, s).wait_send()
-    pg_copy.wait()
-    for copy in wg_copy:
-        copy.wait()
+        for a in range(2):
+            sib_copy(i, a).wait_send()
+    for s in range(2):
+        z_copy(n_z - 2, s).wait_send()
 
 
 def fused(out_grad, routes, gates, pre_acts, down_weight, history):
@@ -536,36 +576,35 @@
     hist = history.shape[2]
     blk = width // n_z
     half = blk // 2
-    wid = blk - half // LANES * LANES
+    big, small, win = split_half(half)
     slots = n_ep * cap
     vmem, anywhere = pl.BlockSpec(memory_space=pltpu.VMEM), pl.BlockSpec(memory_space=pl.ANY)
     pre_grad, wgrad, new_history, gate_grad = pl.pallas_call(
         functools.partial(kernel, n_z, n_ep, cap),
         out_shape=(
-            jax.ShapeDtypeStruct((n_src, cap, 2 * ff), bf16),
-            jax.ShapeDtypeStruct((1, half, ff), f32),
+            pltpu.VMEM((n_src, cap, 2 * ff), bf16),
+            pltpu.VMEM((1, half, ff), f32),
             jax.ShapeDtypeStruct((1, hist), f32),
-            jax.ShapeDtypeStruct((tokens, 2), f32),
+            jax.ShapeDtypeStruct((2, tokens), f32),
         ),
         in_specs=[vmem, vmem, vmem, anywhere, anywhere, anywhere],
-        out_specs=(anywhere, anywhere, vmem, vmem),
+        out_specs=(vmem, vmem, vmem, vmem),
         scratch_shapes=[
             pltpu.VMEM((n_z, tokens, blk), bf16),
             pltpu.VMEM((n_z, ff, blk), bf16),
             pltpu.VMEM((n_src, cap, 2 * ff), bf16),
-            pltpu.VMEM((n_src, cap, 2 * ff), bf16),
             pltpu.VMEM((n_ep, cap, tokens), bf16),
-            pltpu.VMEM((tokens, slots), f32),
+            pltpu.VMEM((n_ep, cap, tokens), f32),
             pltpu.VMEM((n_z, n_ep, cap, blk), bf16),
             pltpu.VMEM((n_z, n_ep, cap, blk), bf16),
-            pltpu.VMEM((n_z, n_ep, cap, wid), bf16),
+            pltpu.VMEM((n_z, 2, n_ep, cap, max(big, win)), bf16),
             pltpu.VMEM((2, slots, ff), bf16),
             pltpu.VMEM((slots, ff), f32),
             pltpu.VMEM((slots, ff), bf16),
-            pltpu.VMEM((wid, 2 * slots), bf16),
+            pltpu.VMEM((max(big, win), 2 * slots), bf16),
             pltpu.VMEM((half, ff), f32),
-            pltpu.VMEM((2, n_z, 2, half // 2, ff), bf16),
-            pltpu.VMEM((n_z - 1, 2, half // 2, ff), bf16),
+            pltpu.VMEM((2, n_z, half, ff), bf16),
+            pltpu.VMEM((n_z - 1, half, ff), bf16),
             pltpu.VMEM((n_ep, cap, LANES), bf16),
             pltpu.VMEM((n_ep, cap, LANES), bf16),
             pltpu.VMEM((n_ep, cap, LANES), f32),
@@ -574,19 +613,17 @@
             pltpu.VMEM((n_ed, 8, LANES), f32),
             pltpu.VMEM((8, LANES), f32),
             pltpu.VMEM((n_ed, 8, LANES), f32),
-            dma((n_z,)),
-            dma((n_z,)),
+            dma((n_z, 3)),
+            dma((n_z, 3)),
             dma((1,)),
-            dma((1,)),
-            dma((2,)),
-            dma((n_z, n_ep)),
-            dma((n_z, n_ep)),
+            dma((n_z, 2, n_ep)),
+            dma((n_z, 2, n_ep)),
             dma((n_ep,)),
             dma((n_ep,)),
             dma((n_ep,)),
             dma((n_ep,)),
-            dma((n_z,)),
-            dma((n_z,)),
+            dma((n_z, 2)),
+            dma((n_z, 2)),
             dma((1,)),
             dma((1,)),
             dma((n_z, 2)),
@@ -603,9 +640,9 @@
             flops=4 * slots * width * ff, bytes_accessed=16 * 1024 * 1024, transcendentals=slots * ff
         ),
     )(
-        routes, gates, history[0], out_grad, pre_acts[0, 0], down_weight
-    )
-    return pre_grad[None, None], wgrad, new_history, gate_grad
+        routes.T, gates.T, history[0], out_grad, pre_acts[0, 0], down_weight
+    )
+    return pre_grad[None, None], wgrad, new_history, gate_grad.T
 
 
 def body(out_grad, routes, gates, pre_acts, down_weight, history):
@@ -620,6 +657,7 @@
         and down_weight.shape[0] == 1
         and width % (n_ed // 2 * LANES) == 0
         and width // n_ed % 64 == 0
+        and lax.axis_size("ep") <= 16
     )
     run = fused if fits else plain
     return run(out_grad, routes, gates, pre_acts, down_weight, history)

time: 101 us -> 96 us (0.950)
  local copies, waits for them, and re-layouts: 9.31 us -> 3.63 us
    unnamed x10 -> x8, local copies, waits for them, and re-layouts: 9.31 us -> 3.63 us
where the time goes in v2:
time: 96 us; the launch traced here: 95.8 us
  Pallas kernels  91.5 us (95%)
  local copies, waits for them, and re-layouts  3.63 us (4%)
    pallas_call x1, Pallas kernels, fused(): pl.pallas_call(functools.partial(kernel, n_z, n_ep, cap), out_shape=(pltp...  91.5 us
    unnamed x8, local copies, waits for them, and re-layouts  3.63 us

profile of v2, /device:TPU:0, one launch (start us, length us, event | category | flops | bytes accessed | tf_op | source)
XLA Modules:
  0.0 95.8 jit_solution(9315662904563385627)
XLA Ops:
  0.6 91.5 %shard_map.93 = (bf16[4,128,2048]{2,1,0:T(8,128)(2,1)S(1)}, f32[1,448,1024]{2,1,0:T(8,128)S(1)}, f32[1,16]{1,0:T(1,128)}, f32[2,128]{1,0:T(2,128)}) custom-call(s32[2,128]{1,0:T(2,128)} %bitcast.9, bf16[2,128]{1,0:T(2,128)(2,1)} %bitcast.10, f32[1,16]{1,0:T(1,128)} %bitcast.11, bf16[128,3584]{1,0:T(8,128)(2,1)} %tok_hbm.1, bf16[4,128,2048]{2,1,0:T(8,128)(2,1)} %bitcast.8, ...), custom_call_target="tpu_custom_call" | custom-call | flops 7516192768 | bytes 16777216 | tf_op jit(solution)/shard_map/pallas_call | solution.py:582
  92.2 1.3 %copy.14 = bf16[1,1,4,128,2048]{4,3,2,1,0:T(8,128)(2,1)} copy(bf16[1,1,4,128,2048]{4,3,2,1,0:T(8,128)(2,1)S(1)} %bitcast.6) | data formatting | bytes 4194304
  93.5 0.0 copy-start.1
  93.5 0.0 copy-start
  93.5 1.2 %copy.15 = f32[1,448,1024]{2,1,0:T(8,128)} copy(f32[1,448,1024]{2,1,0:T(8,128)S(1)} %get-tuple-element.13) | data formatting | bytes 3670016
  94.7 0.0 copy-done.1
  94.7 0.5 copy.16
  95.2 0.0 copy-done
  95.2 0.6 copy.17
Async XLA Ops:
  93.5 1.2 %copy-start.1 = (f32[1,16]{1,0:T(1,128)S(1)}, f32[1,16]{1,0:T(1,128)}, u32[]{:S(2)}) copy-start(f32[1,16]{1,0:T(1,128)} %get-tuple-element.22) | copy-start | bytes 196
  93.5 1.7 %copy-start = (f32[2,128]{1,0:T(2,128)S(1)}, f32[2,128]{1,0:T(2,128)}, u32[]{:S(2)}) copy-start(f32[2,128]{1,0:T(2,128)} %get-tuple-element.11) | copy-start | bytes 3076

commit v3 on v2

--- a/solution.py
+++ b/solution.py
@@ -113,9 +113,9 @@
 
 
 def split_half(half):
-    big = -(-half // (2 * LANES)) * LANES
-    small = half - big
-    return big, small, -(-small // LANES) * LANES
+    whole = max(half // LANES - 1, 0)
+    small = half - whole * LANES
+    return whole, small, -(-small // LANES) * LANES
 
 
 def kernel(
@@ -182,8 +182,10 @@
     sibling = z * 2 + 1 - core
     blk = tok.shape[2]
     half = blk // 2
-    big, small, win = split_half(half)
-    rest = blk - 2 * big
+    whole, small, win = split_half(half)
+    parts = whole + 1
+    lead = 2 * whole * LANES
+    rest = blk - lead
     slots = n_ep * cap
     ff = act.shape[1]
     table = orders(n_z)
@@ -196,7 +198,11 @@
 
     shard = [shard_at(i) for i in range(n_z)]
 
-    pieces = ((0, 0, big), (blk - big, big, big), (big, 2 * big, rest))
+    pieces = []
+    for a in range(whole):
+        pieces.append((a * LANES, 2 * a * LANES, LANES))
+        pieces.append((blk - (a + 1) * LANES, (2 * a + 1) * LANES, LANES))
+    pieces.append((whole * LANES, lead, rest))
 
     def columns(i, begin, count):
         return pl.ds(pl.multiple_of(shard[i] * blk + begin, LANES), count)
@@ -296,7 +302,7 @@
     def peer(d):
         return lax.rem(me + d, n_ep)
 
-    spans = (pl.ds(0, 2 * big), pl.ds(2 * big, rest))
+    spans = [pl.ds(2 * a * LANES, 2 * LANES) for a in range(whole)] + [pl.ds(lead, rest)]
 
     def row_copy(i, a, d, src):
         return to_ep(
@@ -324,22 +330,9 @@
         for d in range(1, n_ep):
             row_copy(i, a, d, me).start()
 
-    dispatch(0, 0)
     for d in range(1, n_ep):
         gate_copy(d, me).start()
-    for d in range(1, n_ed):
-        hist_copy(d, ed).start()
-    hist_all[ed] = hist_mine[...]
-
-    @pl.when(z == 0)
-    def _():
-        recv[0, z] = jnp.zeros(recv.shape[2:], bf16)
-
-    @pl.when(z == n_z - 1)
-    def _():
-        recv[1, z] = jnp.zeros(recv.shape[2:], bf16)
-
-    place_rows(1)
+    dispatch(0, 0)
 
     tile = 32
     pre_in.wait()
@@ -362,15 +355,19 @@
         return to_ed(w2.at[which], w2.at[which], w2_ss.at[0], w2_rs.at[0], sibling)
 
     w2_copy(core).start()
+    for d in range(1, n_ed):
+        hist_copy(d, ed).start()
+    hist_all[ed] = hist_mine[...]
+    place_rows(1)
 
     def window(a, which):
-        if a == 0:
-            return pl.ds(pl.multiple_of(which * big, LANES), big)
-        return pl.ds(pl.multiple_of(2 * big + which * (rest - win), LANES), win)
-
-    heights = (big, small)
-    starts = (0, big)
-    wide = (big, win)
+        if a < whole:
+            return pl.ds(pl.multiple_of((2 * a + which) * LANES, LANES), LANES)
+        return pl.ds(pl.multiple_of(lead + which * (rest - win), LANES), win)
+
+    heights = [LANES] * whole + [small]
+    starts = [a * LANES for a in range(parts)]
+    wide = [LANES] * whole + [win]
 
     def sib_copy(i, a):
         return to_ed(
@@ -378,9 +375,18 @@
             sib_ss.at[i, a], sib_rs.at[i, a], sibling,
         )
 
+    def direction(i):
+        ahead = lax.rem(shard[i] - z + n_z, n_z)
+        right = jnp.where(2 * ahead == n_z, shard[i] > z, 2 * ahead < n_z)
+        before = lax.rem(shard[i] - z + 1 + n_z, n_z)
+        fed_right = jnp.logical_and(2 * before == n_z, jnp.logical_and(z > 0, shard[i] > z))
+        behind = lax.rem(z + 1 - shard[i] + n_z, n_z)
+        fed_left = jnp.logical_and(2 * behind == n_z, jnp.logical_and(z < n_z - 1, shard[i] < z))
+        return right, jnp.where(right, fed_right, fed_left)
+
     def z_copy(i, s):
-        right = shard[i] > z
-        target = jnp.where(right, z + 1, z - 1)
+        right, _ = direction(i)
+        target = lax.rem(jnp.where(right, z + 1, z + n_z - 1), n_z)
         way = jnp.where(right, 0, 1)
         at = pl.ds(starts[s], heights[s])
         return to_ed(
@@ -408,7 +414,7 @@
         rt[0 : wide[a], pl.ds(pl.multiple_of((1 - core) * slots, LANES), slots)] = (
             sib[i, a, :, :, 0 : wide[a]].reshape(slots, wide[a]).T
         )
-        skip = 0 if a == 0 else pl.multiple_of((small - (rest - win)) * core, 16)
+        skip = 0 if a < whole else pl.multiple_of((small - (rest - win)) * core, 16)
 
         @pl.loop(0, ff // n_tile)
         def _(n):
@@ -434,17 +440,16 @@
 
     for i in range(n_z):
         last = i == n_z - 1
-        right = shard[i] > z
+        right, fed = direction(i)
         way = jnp.where(right, 0, 1)
-        fed = jnp.where(right, z > 0, z < n_z - 1)
-        for a in range(2):
+        for a in range(parts):
             for d in range(1, n_ep):
                 row_copy(i, a, d, peer(d)).wait_recv()
-            if i == 0 and a == 0:
-                dispatch(0, 1)
-            if not last and a == 1:
-                dispatch(i + 1, 0)
-                dispatch(i + 1, 1)
+            if i == 0 and a + 1 < parts:
+                dispatch(0, a + 1)
+            if not last and a == parts - 1:
+                for nxt in range(parts):
+                    dispatch(i + 1, nxt)
             part(i, a)
             if not last:
 
@@ -474,7 +479,7 @@
 
         @pl.when(fed)
         def _():
-            for s in range(2):
+            for s in range(parts):
                 z_arrival(way, shard[i], s).wait_recv()
                 send_on(i, s, way)
 
@@ -517,17 +522,10 @@
     gg_out[1:2, :] = value1
 
     amax_mine[...] = jnp.zeros_like(amax_mine)
-    for s in range(2):
-
-        @pl.when(z > 0)
-        def _():
-            z_arrival(0, z, s).wait_recv()
-
-        @pl.when(z < n_z - 1)
-        def _():
-            z_arrival(1, z, s).wait_recv()
-
-        base = core * small if s == 0 else (1 - core) * big
+    for s in range(parts):
+        for way in range(2):
+            z_arrival(way, z, s).wait_recv()
+        base = jnp.where(core == 0, starts[s], half - starts[s] - heights[s])
 
         @pl.loop(0, heights[s] // etile)
         def _(t):
@@ -551,7 +549,7 @@
 
     for d in range(1, n_ep):
         for i in range(n_z):
-            for a in range(2):
+            for a in range(parts):
                 row_copy(i, a, d, me).wait_send()
         gate_copy(d, me).wait_send()
         score_copy(d, me).wait_send()
@@ -560,9 +558,9 @@
         amax_copy(d, ed).wait_send()
     w2_copy(core).wait_send()
     for i in range(n_z):
-        for a in range(2):
+        for a in range(parts):
             sib_copy(i, a).wait_send()
-    for s in range(2):
+    for s in range(parts):
         z_copy(n_z - 2, s).wait_send()
 
 
@@ -576,7 +574,8 @@
     hist = history.shape[2]
     blk = width // n_z
     half = blk // 2
-    big, small, win = split_half(half)
+    whole, small, win = split_half(half)
+    parts, lead = whole + 1, max(LANES, win)
     slots = n_ep * cap
     vmem, anywhere = pl.BlockSpec(memory_space=pltpu.VMEM), pl.BlockSpec(memory_space=pl.ANY)
     pre_grad, wgrad, new_history, gate_grad = pl.pallas_call(
@@ -597,11 +596,11 @@
             pltpu.VMEM((n_ep, cap, tokens), f32),
             pltpu.VMEM((n_z, n_ep, cap, blk), bf16),
             pltpu.VMEM((n_z, n_ep, cap, blk), bf16),
-            pltpu.VMEM((n_z, 2, n_ep, cap, max(big, win)), bf16),
+            pltpu.VMEM((n_z, parts, n_ep, cap, lead), bf16),
             pltpu.VMEM((2, slots, ff), bf16),
             pltpu.VMEM((slots, ff), f32),
             pltpu.VMEM((slots, ff), bf16),
-            pltpu.VMEM((max(big, win), 2 * slots), bf16),
+            pltpu.VMEM((lead, 2 * slots), bf16),
             pltpu.VMEM((half, ff), f32),
             pltpu.VMEM((2, n_z, half, ff), bf16),
             pltpu.VMEM((n_z - 1, half, ff), bf16),
@@ -613,21 +612,21 @@
             pltpu.VMEM((n_ed, 8, LANES), f32),
             pltpu.VMEM((8, LANES), f32),
             pltpu.VMEM((n_ed, 8, LANES), f32),
-            dma((n_z, 3)),
-            dma((n_z, 3)),
+            dma((n_z, 2 * whole + 1)),
+            dma((n_z, 2 * whole + 1)),
             dma((1,)),
-            dma((n_z, 2, n_ep)),
-            dma((n_z, 2, n_ep)),
+            dma((n_z, parts, n_ep)),
+            dma((n_z, parts, n_ep)),
             dma((n_ep,)),
             dma((n_ep,)),
             dma((n_ep,)),
             dma((n_ep,)),
-            dma((n_z, 2)),
-            dma((n_z, 2)),
+            dma((n_z, parts)),
+            dma((n_z, parts)),
             dma((1,)),
             dma((1,)),
-            dma((n_z, 2)),
-            dma((2, n_z, 2)),
+            dma((n_z, parts)),
+            dma((2, n_z, parts)),
             dma((n_ed,)),
             dma((n_ed,)),
             dma((n_ed,)),
@@ -651,7 +650,7 @@
     n_ed = lax.axis_size("ed")
     fits = (
         n_ed % 2 == 0
-        and n_ed > 2
+        and n_ed == 8
         and cap == LANES
         and tokens == LANES
         and down_weight.shape[0] == 1

time: 96 us -> 97 us (1.010)
  Pallas kernels: 91.5 us -> 92.6 us
    pallas_call x1, Pallas kernels: 91.5 us -> 92.6 us  [fused(): pl.pallas_call(functools.partial(kernel, n_z, n_ep, cap), out_shape=(pltp...]
where the time goes in v3:
time: 97 us; the launch traced here: 96.9 us
  Pallas kernels  92.6 us (95%)
  local copies, waits for them, and re-layouts  3.63 us (4%)
    pallas_call x1, Pallas kernels, fused(): pl.pallas_call(functools.partial(kernel, n_z, n_ep, cap), out_shape=(pltp...  92.6 us
    unnamed x8, local copies, waits for them, and re-layouts  3.63 us

profile of v3, /device:TPU:0, one launch (start us, length us, event | category | flops | bytes accessed | tf_op | source)
XLA Modules:
  0.0 96.9 jit_solution(7213430647045567383)
XLA Ops:
  0.6 92.6 %shard_map.93 = (bf16[4,128,2048]{2,1,0:T(8,128)(2,1)S(1)}, f32[1,448,1024]{2,1,0:T(8,128)S(1)}, f32[1,16]{1,0:T(1,128)}, f32[2,128]{1,0:T(2,128)}) custom-call(s32[2,128]{1,0:T(2,128)} %bitcast.9, bf16[2,128]{1,0:T(2,128)(2,1)} %bitcast.10, f32[1,16]{1,0:T(1,128)} %bitcast.11, bf16[128,3584]{1,0:T(8,128)(2,1)} %tok_hbm.1, bf16[4,128,2048]{2,1,0:T(8,128)(2,1)} %bitcast.8, ...), custom_call_target="tpu_custom_call" | custom-call | flops 7516192768 | bytes 16777216 | tf_op jit(solution)/shard_map/pallas_call | solution.py:581
  93.2 1.3 %copy.14 = bf16[1,1,4,128,2048]{4,3,2,1,0:T(8,128)(2,1)} copy(bf16[1,1,4,128,2048]{4,3,2,1,0:T(8,128)(2,1)S(1)} %bitcast.6) | data formatting | bytes 4194304
  94.5 0.0 copy-start.1
  94.5 0.0 copy-start
  94.5 1.2 %copy.15 = f32[1,448,1024]{2,1,0:T(8,128)} copy(f32[1,448,1024]{2,1,0:T(8,128)S(1)} %get-tuple-element.13) | data formatting | bytes 3670016
  95.8 0.0 copy-done.1
  95.8 0.5 copy.16
  96.3 0.0 copy-done
  96.3 0.6 copy.17
Async XLA Ops:
  94.5 1.2 %copy-start.1 = (f32[1,16]{1,0:T(1,128)S(1)}, f32[1,16]{1,0:T(1,128)}, u32[]{:S(2)}) copy-start(f32[1,16]{1,0:T(1,128)} %get-tuple-element.22) | copy-start | bytes 196
  94.5 1.7 %copy-start = (f32[2,128]{1,0:T(2,128)S(1)}, f32[2,128]{1,0:T(2,128)}, u32[]{:S(2)}) copy-start(f32[2,128]{1,0:T(2,128)} %get-tuple-element.11) | copy-start | bytes 3076

commit v4 on v3

--- a/solution.py
+++ b/solution.py
@@ -360,6 +360,14 @@
     hist_all[ed] = hist_mine[...]
     place_rows(1)
 
+    @pl.when(z == 0)
+    def _():
+        recv[0, z] = jnp.zeros(recv.shape[2:], bf16)
+
+    @pl.when(z == n_z - 1)
+    def _():
+        recv[1, z] = jnp.zeros(recv.shape[2:], bf16)
+
     def window(a, which):
         if a < whole:
             return pl.ds(pl.multiple_of((2 * a + which) * LANES, LANES), LANES)
@@ -376,17 +384,12 @@
         )
 
     def direction(i):
-        ahead = lax.rem(shard[i] - z + n_z, n_z)
-        right = jnp.where(2 * ahead == n_z, shard[i] > z, 2 * ahead < n_z)
-        before = lax.rem(shard[i] - z + 1 + n_z, n_z)
-        fed_right = jnp.logical_and(2 * before == n_z, jnp.logical_and(z > 0, shard[i] > z))
-        behind = lax.rem(z + 1 - shard[i] + n_z, n_z)
-        fed_left = jnp.logical_and(2 * behind == n_z, jnp.logical_and(z < n_z - 1, shard[i] < z))
-        return right, jnp.where(right, fed_right, fed_left)
+        right = shard[i] > z
+        return right, jnp.where(right, z > 0, z < n_z - 1)
 
     def z_copy(i, s):
         right, _ = direction(i)
-        target = lax.rem(jnp.where(right, z + 1, z + n_z - 1), n_z)
+        target = jnp.where(right, z + 1, z - 1)
         way = jnp.where(right, 0, 1)
         at = pl.ds(starts[s], heights[s])
         return to_ed(
@@ -523,8 +526,15 @@
 
     amax_mine[...] = jnp.zeros_like(amax_mine)
     for s in range(parts):
-        for way in range(2):
-            z_arrival(way, z, s).wait_recv()
+
+        @pl.when(z > 0)
+        def _():
+            z_arrival(0, z, s).wait_recv()
+
+        @pl.when(z < n_z - 1)
+        def _():
+            z_arrival(1, z, s).wait_recv()
+
         base = jnp.where(core == 0, starts[s], half - starts[s] - heights[s])
 
         @pl.loop(0, heights[s] // etile)
@@ -583,8 +593,8 @@
         out_shape=(
             pltpu.VMEM((n_src, cap, 2 * ff), bf16),
             pltpu.VMEM((1, half, ff), f32),
-            jax.ShapeDtypeStruct((1, hist), f32),
-            jax.ShapeDtypeStruct((2, tokens), f32),
+            pltpu.VMEM((1, hist), f32),
+            pltpu.VMEM((2, tokens), f32),
         ),
         in_specs=[vmem, vmem, vmem, anywhere, anywhere, anywhere],
         out_specs=(vmem, vmem, vmem, vmem),
@@ -650,7 +660,7 @@
     n_ed = lax.axis_size("ed")
     fits = (
         n_ed % 2 == 0
-        and n_ed == 8
+        and n_ed > 2
         and cap == LANES
         and tokens == LANES
         and down_weight.shape[0] == 1

time: 97 us -> 92.7 us (0.956)
  Pallas kernels: 92.6 us -> 88.3 us
    pallas_call x1, Pallas kernels: 92.6 us -> 88.3 us  [fused(): pl.pallas_call(functools.partial(kernel, n_z, n_ep, cap), out_shape=(pltp...]
    unnamed x8 -> x4, local copies, waits for them, and re-layouts: 3.63 us -> 3.62 us
where the time goes in v4:
time: 92.7 us; the launch traced here: 92.5 us
  Pallas kernels  88.3 us (95%)
  local copies, waits for them, and re-layouts  3.62 us (4%)
    pallas_call x1, Pallas kernels, fused(): pl.pallas_call(functools.partial(kernel, n_z, n_ep, cap), out_shape=(pltp...  88.3 us
    unnamed x4, local copies, waits for them, and re-layouts  3.62 us

profile of v4, /device:TPU:0, one launch (start us, length us, event | category | flops | bytes accessed | tf_op | source)
XLA Modules:
  0.0 92.5 jit_solution(7614768308935502805)
XLA Ops:
  0.6 88.3 %shard_map.93 = (bf16[4,128,2048]{2,1,0:T(8,128)(2,1)S(1)}, f32[1,448,1024]{2,1,0:T(8,128)S(1)}, f32[1,16]{1,0:T(1,128)S(1)}, f32[2,128]{1,0:T(2,128)S(1)}) custom-call(s32[2,128]{1,0:T(2,128)} %bitcast.9, bf16[2,128]{1,0:T(2,128)(2,1)} %bitcast.10, f32[1,16]{1,0:T(1,128)} %bitcast.11, bf16[128,3584]{1,0:T(8,128)(2,1)} %tok_hbm.1, ...), custom_call_target="tpu_custom_call" | custom-call | flops 7516192768 | bytes 16777216 | tf_op jit(solution)/shard_map/pallas_call | solution.py:591
  88.9 1.3 %copy.14 = bf16[1,1,4,128,2048]{4,3,2,1,0:T(8,128)(2,1)} copy(bf16[1,1,4,128,2048]{4,3,2,1,0:T(8,128)(2,1)S(1)} %bitcast.6) | data formatting | bytes 4194304
  90.2 0.5 copy.16
  90.8 0.6 copy.17
  91.3 1.2 %copy.15 = f32[1,448,1024]{2,1,0:T(8,128)} copy(f32[1,448,1024]{2,1,0:T(8,128)S(1)} %get-tuple-element.13) | data formatting | bytes 3670016
